TPU v7x, 32 devices: a whole 2x2x4 slice. The times are simulated.
32 devices in a mesh: flow: 2 (over x), col: 4 (over y, core), row: 4 (over z).
Axes of the slice: x: 2, y: 2, z: 4, core: 2. Of those that a mesh axis runs over, the one named last changes fastest.
Arguments:
- forcing: float32 [5, 12, 48, 768], P(None, 'flow', 'col', 'row'), may hold values from -6 to 6
- previous: float32 [5, 12, 48, 768], P(None, 'flow', 'col', 'row'), may hold values from -6 to 6
- element_diagonal_shift: float32 [2, 8, 128], P('flow', 'col', 'row'), may hold values from 0.5 to 4
- eigen_bases: float32 [3, 6, 6], replicated, may hold values from -1 to 1, as said below
- eigen_values: float32 [3, 6], replicated, may hold values from 0.5 to 8
- observers: float32 [3, 256], replicated, may hold values from 8 to 30
- panel_points: float32 [3, 1024], P(None, ('flow', 'col', 'row')), may hold values from -2 to 2
- surface_history: float32 [4, 15, 1024], P(None, None, ('flow', 'col', 'row')), may hold values from -6 to 6
Outputs:
- new_state: float32 [5, 12, 48, 768], P(None, 'flow', 'col', 'row')
- spectra: float32 [2, 16, 256], P(None, None, 'row')
Inputs may be any that keep to these rules, and one draw needn't show every extreme that they name: Each eigen_bases[d] is an orthogonal matrix.
All inputs are finite; a program needn't handle non-finite values.
Results may differ from a plain program's by a relative error of at most 0.0003.
Values sent between devices are 32-bit elements; how exact they have to be, the bound alone decides.
A program may use at most 64 MiB of HBM per device.

v0:
```python
import math
import jax
import jax.numpy as jnp
from jax import lax
from jax.sharding import PartitionSpec as P

P_SIZE = 6
SWEEPS = 2
NT = 16
NF = 16
HIGH = lax.Precision.HIGHEST
OMEGA = 0.8
TAU = 0.5
KMAX = 2.0


def with_halo(x, sides, width):
    for axis, dim in sides:
        size, length = (lax.axis_size(axis), x.shape[dim])
        up = [(i, (i + 1) % size) for i in range(size - 1)]
        down = [(j, i) for i, j in up]
        last = lax.slice_in_dim(x, length - width, length, axis=dim)
        first = lax.slice_in_dim(x, 0, width, axis=dim)
        before = lax.ppermute(last, axis, up)
        after = lax.ppermute(first, axis, down)
        x = jnp.concatenate([before, x, after], axis=dim)
    return x


def contract_small(field, matrix, which):
    extent = field.shape
    count = extent[which]
    blocked = field.reshape(extent[:which] + (count // P_SIZE, P_SIZE) + extent[which + 1 :])
    blocked = jnp.moveaxis(blocked, which + 1, -1)
    result = jnp.einsum("...p,qp->...q", blocked, matrix, precision=HIGH)
    result = jnp.moveaxis(result, -1, which + 1)
    return result.reshape(extent)


def contract_last(field, wide_matrix):
    extent = field.shape
    group = wide_matrix.shape[0]
    blocked = field.reshape(extent[0], extent[1], extent[2], extent[3] // group, group)
    result = jnp.einsum("cxybg,hg->cxybh", blocked, wide_matrix, precision=HIGH)
    return result.reshape(extent)


def face_masks(count):
    index = jnp.arange(count) % P_SIZE
    return ((index == P_SIZE - 1).astype(jnp.float32), (index == 0).astype(jnp.float32))


def far_terms(observers, points, source_re, source_im):
    offsets = observers[:, :, None] - points[:, None, :]
    radius = jnp.sqrt(jnp.sum(offsets * offsets, axis=0))
    unit_dir = offsets / radius[None]
    freqs = source_re.shape[1]
    wavenum = (KMAX * (jnp.arange(freqs, dtype=jnp.float32) + 0.5) / freqs)[:, None, None]
    along_re = (
        unit_dir[0][None] * source_re[1][:, None, :]
        + unit_dir[1][None] * source_re[2][:, None, :]
        + unit_dir[2][None] * source_re[3][:, None, :]
    )
    along_im = (
        unit_dir[0][None] * source_im[1][:, None, :]
        + unit_dir[1][None] * source_im[2][:, None, :]
        + unit_dir[2][None] * source_im[3][:, None, :]
    )
    inverse_matrix = 1.0 / radius[None]
    term_re = -wavenum * (source_im[0][:, None, :] + along_im) + along_re * inverse_matrix
    term_im = wavenum * (source_re[0][:, None, :] + along_re) + along_im * inverse_matrix
    phases = wavenum * radius[None]
    amplitude = inverse_matrix / (4.0 * math.pi)
    green_re = amplitude * jnp.cos(phases)
    green_im = -amplitude * jnp.sin(phases)
    total_re = jnp.sum(green_re * term_re - green_im * term_im, axis=2)
    total_im = jnp.sum(green_re * term_im + green_im * term_re, axis=2)
    return jnp.stack([total_re, total_im])


def transform(samples):
    times = jnp.arange(NT, dtype=jnp.float32)
    omegas = math.pi * (jnp.arange(NF, dtype=jnp.float32) + 0.5) / NF
    cos_table = jnp.cos(omegas[:, None] * times[None, :])
    sin_table = jnp.sin(omegas[:, None] * times[None, :])
    source_re = jnp.einsum("fn,cnp->cfp", cos_table, samples, precision=HIGH)
    source_im = -jnp.einsum("fn,cnp->cfp", sin_table, samples, precision=HIGH)
    return (source_re, source_im)


def on_device(
    forcing,
    previous,
    element_diagonal_shift,
    eigen_bases,
    eigen_values,
    observers,
    panel_points,
    surface_history,
):
    extent = forcing.shape
    stiffness = [
        jnp.dot(
            eigen_bases[axis_num] * eigen_values[axis_num][None, :],
            eigen_bases[axis_num].T,
            precision=HIGH,
        )
        for axis_num in range(3)
    ]
    group = P_SIZE * math.gcd(extent[3] // P_SIZE, 64)
    identity = jnp.eye(group // P_SIZE, dtype=jnp.float32)
    wide_stiff = jnp.kron(identity, stiffness[2])
    wide_forward = jnp.kron(identity, eigen_bases[2].T)
    wide_back = jnp.kron(identity, eigen_bases[2])
    shift_nodes = jnp.repeat(
        jnp.repeat(jnp.repeat(element_diagonal_shift, P_SIZE, 0), P_SIZE, 1), P_SIZE, 2
    )
    denominator = (
        shift_nodes
        + jnp.tile(eigen_values[0], extent[1] // P_SIZE)[:, None, None]
        + jnp.tile(eigen_values[1], extent[2] // P_SIZE)[None, :, None]
        + jnp.tile(eigen_values[2], extent[3] // P_SIZE)[None, None, :]
    )
    high_x, low_x = face_masks(extent[1])
    high_y, low_y = face_masks(extent[2])
    high_z, low_z = face_masks(extent[3])
    state = previous
    for sweep in range(SWEEPS):
        apply_result = shift_nodes[None] * state + contract_small(state, stiffness[0], 1)
        apply_result = apply_result + contract_small(state, stiffness[1], 2)
        padded = with_halo(state, (("flow", 1), ("col", 2), ("row", 3)), 1)
        next_x = padded[:, 2:, 1:-1, 1:-1]
        prev_x = padded[:, :-2, 1:-1, 1:-1]
        next_y = padded[:, 1:-1, 2:, 1:-1]
        prev_y = padded[:, 1:-1, :-2, 1:-1]
        next_z = padded[:, 1:-1, 1:-1, 2:]
        prev_z = padded[:, 1:-1, 1:-1, :-2]
        result = high_x[None, :, None, None] * next_x + low_x[None, :, None, None] * prev_x
        result = result + high_y[None, None, :, None] * next_y + low_y[None, None, :, None] * prev_y
        residual = (
            forcing
            - (apply_result + contract_last(state, wide_stiff))
            + TAU
            * (result + high_z[None, None, None, :] * next_z + low_z[None, None, None, :] * prev_z)
        )
        block_result = contract_small(residual, eigen_bases[0].T, 1)
        block_result = contract_small(block_result, eigen_bases[1].T, 2)
        block_result = contract_last(block_result, wide_forward) / denominator[None]
        block_result = contract_small(block_result, eigen_bases[0], 1)
        block_result = contract_small(block_result, eigen_bases[1], 2)
        state = state + OMEGA * contract_last(block_result, wide_back)
    own_panels = panel_points.shape[1]
    newest = state[:4, 0, 0, :own_panels]
    surface_samples = jnp.concatenate([surface_history, newest[:, None, :]], axis=1)
    rows = lax.axis_size("row")
    count = observers.shape[1] // rows
    points, samples = (
        lax.all_gather(panel_points, "row", axis=1, tiled=True),
        lax.all_gather(surface_samples, "row", axis=2, tiled=True),
    )
    source_re, source_im = transform(samples)
    own_obs = lax.dynamic_slice_in_dim(observers, lax.axis_index("row") * count, count, 1)
    partial_sums = far_terms(own_obs, points, source_re, source_im)
    spectra = lax.psum(partial_sums, ("flow", "col"))
    return (state, spectra)


def solution(mesh):
    return jax.shard_map(
        on_device,
        mesh=mesh,
        in_specs=(
            P(None, "flow", "col", "row"),
            P(None, "flow", "col", "row"),
            P("flow", "col", "row"),
            P(),
            P(),
            P(),
            P(None, ("flow", "col", "row")),
            P(None, None, ("flow", "col", "row")),
        ),
        out_specs=(P(None, "flow", "col", "row"), P(None, None, "row")),
        check_vma=False,
    )
```

profile of v0, /device:TPU:0, one launch (start us, length us, event | category | flops | bytes accessed | tf_op | source)
XLA Modules:
  0.0 143.8 jit_solution(3606890502460777156)
XLA Ops:
  0.6 0.9 fusion.168
  1.7 1.3 collective-permute-start
  3.0 4.8 %collective-permute-start.1 = (f32[5,1,12,192]{3,1,2,0:T(1,128)S(1)}, f32[5,1,12,192]{3,1,2,0:T(1,128)S(1)}, u32[]{:S(2)}, u32[]{:S(2)}) collective-permute-start(f32[5,1,12,192]{3,1,2,0:T(1,128)S(1)} %copy.139), channel_id=1, source_target_pairs={{0,16},{1,17},{2,18},{3,19},{4,20},{5,21},{6,22},{7,23},{8,24},{9,... | collective-permute-start | bytes 138248 | tf_op jit(solution)/shard_map/ppermute | solution.py:24
  7.9 1.3 copy.153
  9.2 0.7 slice_bitcast_fusion.12
  10.0 0.8 slice_bitcast_fusion.15
  10.8 0.9 fusion.131
  11.7 4.9 %broadcast_multiply_fusion = (f32[32,6,32,6]{3,2,1,0:T(8,128)}, f32[32,6,32,6]{3,2,1,0:T(8,128)}, f32[32,6,32,6]{3,2,1,0:T(8,128)}) fusion(f32[6,6]{1,0:T(8,128)S(1)} %get-tuple-element.42, f32[32,32]{1,0:T(8,128)S(1)} %fusion.118, f32[6,6]{1,0:T(8,128)S(1)} %copy.146, f32[6,6]{1,0:T(8,128)S(1)} %fusion.131), kind=kLoop, calls=%fused_computation | loop fusion | flops 110592 | bytes 446896 | tf_op jit(solution)/shard_map/jit(kron)/mul | solution.py:114
  16.6 3.9 %reshape.301 = f32[192,192,1,1]{1,0,2,3:T(8,128)S(1)} reshape(f32[32,6,32,6]{3,2,1,0:T(8,128)} %get-tuple-element.41) | data formatting | bytes 294912 | tf_op jit(solution)/shard_map/jit(kron)/mul | solution.py:112
  20.6 0.7 convolution_bitcast_fusion.6
  21.4 0.6 convolution_bitcast_fusion.7
  22.1 0.2 copy.134
  22.5 0.1 broadcast_in_dim.21
  22.9 13.2 %all-gather = f32[4,32,3]{1,2,0:T(4,128)S(1)} all-gather(f32[1,32,3]{1,2,0:T(4,128)S(1)} %bitcast.282), channel_id=1, replica_groups=mesh['flow'=2,'col'=4,'row'=4] {'row'}, dimensions={0}, use_global_device_ids=true | all-gather | bytes 1920 | tf_op jit(solution)/shard_map/all_gather | solution.py:158
  36.4 0.7 broadcast_multiply_fusion.3
  37.2 0.6 slice_bitcast_fusion.2
  37.8 0.7 add_add_fusion
  38.5 1.1 fusion.3
  39.7 1.3 collective-permute-start.2
  41.0 3.0 %collective-permute-start.3 = (f32[5,8,1,192]{3,1,2,0:T(8,128)S(1)}, f32[5,8,1,192]{3,1,2,0:T(8,128)S(1)}, u32[]{:S(2)}, u32[]{:S(2)}) collective-permute-start(f32[5,8,1,192]{3,1,2,0:T(8,128)S(1)} %get-tuple-element.14), channel_id=1, source_target_pairs={{0,4},{4,8},{8,12},{1,5},{5,9},{9,13},{2,6},{6,10},{10,14},{3,7},{... | collective-permute-start | bytes 92168 | tf_op jit(solution)/shard_map/ppermute | solution.py:24
  44.1 0.8 collective-permute-done.3
  44.9 0.2 pad_maximum_fusion
  45.1 0.1 fusion.166
  45.3 4.2 %collective-permute-start.5 = (f32[5,8,14,1]{3,1,2,0:T(8,128)S(1)}, f32[5,8,14,1]{3,1,2,0:T(8,128)}, u32[]{:S(2)}, u32[]{:S(2)}) collective-permute-start(f32[5,8,14,1]{3,1,2,0:T(8,128)S(1)} %get-tuple-element.19), channel_id=1, source_target_pairs={{0,1},{1,2},{2,3},{4,5},{5,6},{6,7},{8,9},{9,10},{10,11},{12,13},{... | collective-permute-start | bytes 6728 | tf_op jit(solution)/shard_map/ppermute | solution.py:24
  49.5 1.5 %collective-permute-start.4 = (f32[5,8,14,1]{3,1,2,0:T(8,128)S(1)}, f32[5,8,14,1]{3,1,2,0:T(8,128)}, u32[]{:S(2)}, u32[]{:S(2)}) collective-permute-start(f32[5,8,14,1]{3,1,2,0:T(8,128)S(1)} %get-tuple-element.18), channel_id=1, source_target_pairs={{1,0},{2,1},{3,2},{5,4},{6,5},{7,6},{9,8},{10,9},{11,10},{13,12},{... | collective-permute-start | bytes 6728 | tf_op jit(solution)/shard_map/ppermute | solution.py:25
  51.0 3.9 %reshape.304 = f32[192,192,1,1]{1,0,2,3:T(8,128)S(1)} reshape(f32[32,6,32,6]{3,2,1,0:T(8,128)} %get-tuple-element.40) | data formatting | bytes 294912 | tf_op jit(solution)/shard_map/jit(kron)/mul | solution.py:113
  54.8 3.9 %reshape.307 = f32[192,192,1,1]{1,0,2,3:T(8,128)S(1)} reshape(f32[32,6,32,6]{3,2,1,0:T(8,128)} %get-tuple-element.39) | data formatting | bytes 294912 | tf_op jit(solution)/shard_map/jit(kron)/mul | solution.py:114
  58.8 2.2 %collective-permute-done.4 = f32[5,8,14,1]{3,1,2,0:T(8,128)} collective-permute-done((f32[5,8,14,1]{3,1,2,0:T(8,128)S(1)}, f32[5,8,14,1]{3,1,2,0:T(8,128)}, u32[]{:S(2)}, u32[]{:S(2)}) %collective-permute-start.4) | collective-permute-done | bytes 2272 | tf_op jit(solution)/shard_map/ppermute | solution.py:25
  61.0 2.7 %fusion.55 = f32[5,12,192,6]{2,3,1,0:T(8,128)S(1)} fusion(f32[5,6,12,192]{3,1,2,0:T(8,128)S(1)} %fusion.3, f32[5,8,14,1]{3,1,2,0:T(8,128)} %collective-permute-done.5, f32[5,8,1,192]{3,1,2,0:T(8,128)S(1)} %collective-permute-done.2, f32[5,8,1,192]{3,1,2,0:T(8,128)S(1)} %collective-permute-done.3, f32[5,1,12,192]{3,1,2,0:T(1,128)S(1)} %collective-permute-done, ...), kind=kOutput, calls=%fused_computation.96 | convolution fusion | flops 7119360 | bytes 1476992 | tf_op jit(solution)/shard_map/...p,qp->...q/dot_general | solution.py:35
  63.8 0.6 convolution_bitcast_fusion.5
  64.5 0.2 copy.145
  64.7 0.6 fusion.11
  65.3 0.8 fusion.90
  66.1 0.6 convolution_bitcast_fusion.4
  66.7 0.2 copy.150
  66.9 0.8 fusion.10
  67.9 1.3 collective-permute-start.6
  69.2 4.5 %collective-permute-start.7 = (f32[5,1,12,192]{3,1,2,0:T(1,128)S(1)}, f32[5,1,12,192]{3,1,2,0:T(1,128)S(1)}, u32[]{:S(2)}, u32[]{:S(2)}) collective-permute-start(f32[5,1,12,192]{3,1,2,0:T(1,128)S(1)} %get-tuple-element.20), channel_id=1, source_target_pairs={{0,16},{1,17},{2,18},{3,19},{4,20},{5,21},{6,22},{7,23},{8,24},{9,... | collective-permute-start | bytes 138248 | tf_op jit(solution)/shard_map/ppermute | solution.py:24
  73.7 0.6 fusion.114
  74.4 1.2 collective-permute-done.7
  75.6 1.3 collective-permute-start.8
  76.9 3.3 %collective-permute-start.9 = (f32[5,8,1,192]{3,1,2,0:T(8,128)S(1)}, f32[5,8,1,192]{3,1,2,0:T(8,128)S(1)}, u32[]{:S(2)}, u32[]{:S(2)}) collective-permute-start(f32[5,8,1,192]{3,1,2,0:T(8,128)S(1)} %get-tuple-element.12), channel_id=1, source_target_pairs={{0,4},{4,8},{8,12},{1,5},{5,9},{9,13},{2,6},{6,10},{10,14},{3,7},{... | collective-permute-start | bytes 92168 | tf_op jit(solution)/shard_map/ppermute | solution.py:24
  80.2 0.6 convolution_bitcast_fusion.2
  80.8 0.2 copy.155
  81.1 0.2 pad_maximum_fusion.1
  81.4 2.4 %collective-permute-start.11 = (f32[5,8,14,1]{3,1,2,0:T(8,128)S(1)}, f32[5,8,14,1]{3,1,2,0:T(8,128)S(1)}, u32[]{:S(2)}, u32[]{:S(2)}) collective-permute-start(f32[5,8,14,1]{3,1,2,0:T(8,128)S(1)} %get-tuple-element.17), channel_id=1, source_target_pairs={{0,1},{1,2},{2,3},{4,5},{5,6},{6,7},{8,9},{9,10},{10,11},{12,13},{... | collective-permute-start | bytes 6728 | tf_op jit(solution)/shard_map/ppermute | solution.py:24
  83.8 1.3 collective-permute-start.10
  85.1 0.8 fusion.7
  85.9 2.9 %collective-permute-done.11 = f32[5,8,14,1]{3,1,2,0:T(8,128)S(1)} collective-permute-done((f32[5,8,14,1]{3,1,2,0:T(8,128)S(1)}, f32[5,8,14,1]{3,1,2,0:T(8,128)S(1)}, u32[]{:S(2)}, u32[]{:S(2)}) %collective-permute-start.11) | collective-permute-done | bytes 2272 | tf_op jit(solution)/shard_map/ppermute | solution.py:24
  88.8 4.7 %collective-permute-done.10 = f32[5,8,14,1]{3,1,2,0:T(8,128)S(1)} collective-permute-done((f32[5,8,14,1]{3,1,2,0:T(8,128)S(1)}, f32[5,8,14,1]{3,1,2,0:T(8,128)S(1)}, u32[]{:S(2)}, u32[]{:S(2)}) %collective-permute-start.10) | collective-permute-done | bytes 2272 | tf_op jit(solution)/shard_map/ppermute | solution.py:25
  93.5 1.7 %fusion.28 = f32[5,12,192,6]{2,3,1,0:T(8,128)S(1)} fusion(f32[5,6,12,192]{3,1,2,0:T(8,128)S(1)} %fusion.7, f32[5,8,14,1]{3,1,2,0:T(8,128)S(1)} %collective-permute-done.11, f32[5,8,1,192]{3,1,2,0:T(8,128)S(1)} %collective-permute-done.8, f32[5,8,1,192]{3,1,2,0:T(8,128)S(1)} %collective-permute-done.9, f32[5,1,12,192]{3,1,2,0:T(1,128)S(1)} %collective-permute-done.6, ...), kind=kOutput, calls=%fused_computation.57 | convolution fusion | flops 7119360 | bytes 2045952 | tf_op jit(solution)/shard_map/...p,qp->...q/dot_general | solution.py:35
  95.2 0.6 convolution_bitcast_fusion.1
  95.8 0.2 copy.162
  96.0 0.6 fusion.9
  96.7 0.8 fusion.84
  97.5 0.6 convolution_bitcast_fusion
  98.1 0.2 copy.166
  98.3 0.7 fusion.8
  99.0 0.9 copy.174
  100.2 14.4 %all_gather.7 = f32[4,16,128]{1,0,2:T(4,128)S(1)} all-gather(f32[4,16,32]{1,0,2:T(4,128)S(1)} %pad_maximum_fusion.62), channel_id=1, replica_groups=mesh['flow'=2,'col'=4,'row'=4] {'row'}, dimensions={2}, use_global_device_ids=true | all-gather | bytes 40960 | tf_op jit(solution)/shard_map/all_gather | solution.py:159
  114.7 0.3 convolution_bitcast_fusion.9
  115.0 0.3 fusion.12
  115.4 2.7 %fusion.17 = (f32[16,64]{1,0:T(8,128)S(1)}, f32[16,64]{1,0:T(8,128)S(1)}) fusion(f32[16,128]{1,0:T(8,128)S(1)} %get-tuple-element.36, f32[64,128]{1,0:T(8,128)S(1)} %copy-done.6, f32[64,128]{1,0:T(8,128)S(1)} %copy-done.7, f32[16,128]{1,0:T(8,128)S(1)} %get-tuple-element.37, f32[16,128]{1,0:T(8,128)S(1)} %get-tuple-element.38, ...), kind=kLoop, calls=%fused_computation.41 | loop fusion | flops 3799040 | bytes 303232 | tf_op jit(solution)/shard_map/reduce_sum | solution.py:76
  118.1 25.7 %psum.7 = f32[2,16,64]{2,1,0:T(8,128)} all-reduce(f32[2,16,64]{2,1,0:T(8,128)S(1)} %pad_maximum_fusion.69), channel_id=1, replica_groups=mesh['flow'=2,'col'=4,'row'=4] {'flow','col'}, use_global_device_ids=true, to_apply=%region_3.4 | all-reduce | flops 2048 | bytes 16384 | tf_op jit(solution)/shard_map/psum | solution.py:164
  (70 shorter events, 2.0 us)
Async XLA Ops:
  0.6 35.6 %copy-start = (f32[3,256]{1,0:T(4,128)S(1)}, f32[3,256]{1,0:T(4,128)}, u32[]{:S(2)}) copy-start(f32[3,256]{1,0:T(4,128)} %param.13) | copy-start | bytes 9220
  1.7 38.0 %collective-permute-start = (f32[5,1,12,192]{3,1,2,0:T(1,128)S(1)}, f32[5,1,12,192]{3,1,2,0:T(1,128)S(1)}, u32[]{:S(2)}, u32[]{:S(2)}) collective-permute-start(f32[5,1,12,192]{3,1,2,0:T(1,128)S(1)} %copy.137), channel_id=1, source_target_pairs={{16,0},{17,1},{18,2},{19,3},{20,4},{21,5},{22,6},{23,7},{24,8},{25... | collective-permute-start | bytes 138248 | tf_op jit(solution)/shard_map/ppermute | solution.py:25
  3.0 36.6 %collective-permute-start.1 = (f32[5,1,12,192]{3,1,2,0:T(1,128)S(1)}, f32[5,1,12,192]{3,1,2,0:T(1,128)S(1)}, u32[]{:S(2)}, u32[]{:S(2)}) collective-permute-start(f32[5,1,12,192]{3,1,2,0:T(1,128)S(1)} %copy.139), channel_id=1, source_target_pairs={{0,16},{1,17},{2,18},{3,19},{4,20},{5,21},{6,22},{7,23},{8,24},{9,... | collective-permute-start | bytes 138248 | tf_op jit(solution)/shard_map/ppermute | solution.py:24
  16.6 4.0 %copy-start.1 = (f32[5,6,12,192]{3,2,1,0:T(8,128)S(1)}, f32[5,6,12,192]{3,2,1,0:T(8,128)}, u32[]{:S(2)}) copy-start(f32[5,6,12,192]{3,2,1,0:T(8,128)} %param.9) | copy-start | bytes 829444
  16.6 4.7 %copy-start.3 = (f32[3,6,6]{2,1,0:T(8,128)S(1)}, f32[3,6,6]{2,1,0:T(8,128)}, u32[]{:S(2)}) copy-start(f32[3,6,6]{2,1,0:T(8,128)} %param.11) | copy-start | bytes 1300
  16.6 5.8 %copy-start.13 = (f32[1,2,32]{2,1,0:T(2,128)S(1)}, f32[1,2,32]{2,1,0:T(2,128)}, u32[]{:S(2)}) copy-start(f32[1,2,32]{2,1,0:T(2,128)} %param.10) | copy-start | bytes 772
  16.6 6.3 %copy-start.12 = (f32[3,32]{1,0:T(4,128)S(1)}, f32[3,32]{1,0:T(4,128)}, u32[]{:S(2)}) copy-start(f32[3,32]{1,0:T(4,128)} %param.14) | copy-start | bytes 1156
  16.6 21.9 %copy-start.2 = (f32[5,6,12,192]{3,2,1,0:T(8,128)S(1)}, f32[5,6,12,192]{3,2,1,0:T(8,128)}, u32[]{:S(2)}) copy-start(f32[5,6,12,192]{3,2,1,0:T(8,128)} %param.8) | copy-start | bytes 829444
  39.7 4.4 %collective-permute-start.2 = (f32[5,8,1,192]{3,1,2,0:T(8,128)S(1)}, f32[5,8,1,192]{3,1,2,0:T(8,128)S(1)}, u32[]{:S(2)}, u32[]{:S(2)}) collective-permute-start(f32[5,8,1,192]{3,1,2,0:T(8,128)S(1)} %get-tuple-element.15), channel_id=1, source_target_pairs={{4,0},{8,4},{12,8},{5,1},{9,5},{13,9},{6,2},{10,6},{14,10},{7,3},{... | collective-permute-start | bytes 92168 | tf_op jit(solution)/shard_map/ppermute | solution.py:25
  41.0 3.9 %collective-permute-start.3 = (f32[5,8,1,192]{3,1,2,0:T(8,128)S(1)}, f32[5,8,1,192]{3,1,2,0:T(8,128)S(1)}, u32[]{:S(2)}, u32[]{:S(2)}) collective-permute-start(f32[5,8,1,192]{3,1,2,0:T(8,128)S(1)} %get-tuple-element.14), channel_id=1, source_target_pairs={{0,4},{4,8},{8,12},{1,5},{5,9},{9,13},{2,6},{6,10},{10,14},{3,7},{... | collective-permute-start | bytes 92168 | tf_op jit(solution)/shard_map/ppermute | solution.py:24
  45.3 13.6 %collective-permute-start.5 = (f32[5,8,14,1]{3,1,2,0:T(8,128)S(1)}, f32[5,8,14,1]{3,1,2,0:T(8,128)}, u32[]{:S(2)}, u32[]{:S(2)}) collective-permute-start(f32[5,8,14,1]{3,1,2,0:T(8,128)S(1)} %get-tuple-element.19), channel_id=1, source_target_pairs={{0,1},{1,2},{2,3},{4,5},{5,6},{6,7},{8,9},{9,10},{10,11},{12,13},{... | collective-permute-start | bytes 6728 | tf_op jit(solution)/shard_map/ppermute | solution.py:24
  49.5 11.6 %collective-permute-start.4 = (f32[5,8,14,1]{3,1,2,0:T(8,128)S(1)}, f32[5,8,14,1]{3,1,2,0:T(8,128)}, u32[]{:S(2)}, u32[]{:S(2)}) collective-permute-start(f32[5,8,14,1]{3,1,2,0:T(8,128)S(1)} %get-tuple-element.18), channel_id=1, source_target_pairs={{1,0},{2,1},{3,2},{5,4},{6,5},{7,6},{9,8},{10,9},{11,10},{13,12},{... | collective-permute-start | bytes 6728 | tf_op jit(solution)/shard_map/ppermute | solution.py:25
  51.0 7.7 %copy-start.11 = (f32[4,15,32]{2,0,1:T(4,128)S(1)}, f32[4,15,32]{2,0,1:T(4,128)}, u32[]{:S(2)}) copy-start(f32[4,15,32]{2,0,1:T(4,128)} %param.15) | copy-start | bytes 23044
  61.0 3.6 %copy-start.4 = (f32[6,12,192]{2,1,0:T(8,128)S(1)}, f32[6,12,192]{2,1,0:T(8,128)}, u32[]{:S(2)}) copy-start(f32[6,12,192]{2,1,0:T(8,128)} %add_add_fusion) | copy-start | bytes 165892
  67.9 6.5 %collective-permute-start.6 = (f32[5,1,12,192]{3,1,2,0:T(1,128)S(1)}, f32[5,1,12,192]{3,1,2,0:T(1,128)S(1)}, u32[]{:S(2)}, u32[]{:S(2)}) collective-permute-start(f32[5,1,12,192]{3,1,2,0:T(1,128)S(1)} %get-tuple-element.21), channel_id=1, source_target_pairs={{16,0},{17,1},{18,2},{19,3},{20,4},{21,5},{22,6},{23,7},{24,8},{25... | collective-permute-start | bytes 138248 | tf_op jit(solution)/shard_map/ppermute | solution.py:25
  69.2 6.4 %collective-permute-start.7 = (f32[5,1,12,192]{3,1,2,0:T(1,128)S(1)}, f32[5,1,12,192]{3,1,2,0:T(1,128)S(1)}, u32[]{:S(2)}, u32[]{:S(2)}) collective-permute-start(f32[5,1,12,192]{3,1,2,0:T(1,128)S(1)} %get-tuple-element.20), channel_id=1, source_target_pairs={{0,16},{1,17},{2,18},{3,19},{4,20},{5,21},{6,22},{7,23},{8,24},{9,... | collective-permute-start | bytes 138248 | tf_op jit(solution)/shard_map/ppermute | solution.py:24
  75.6 5.4 %collective-permute-start.8 = (f32[5,8,1,192]{3,1,2,0:T(8,128)S(1)}, f32[5,8,1,192]{3,1,2,0:T(8,128)S(1)}, u32[]{:S(2)}, u32[]{:S(2)}) collective-permute-start(f32[5,8,1,192]{3,1,2,0:T(8,128)S(1)} %get-tuple-element.13), channel_id=1, source_target_pairs={{4,0},{8,4},{12,8},{5,1},{9,5},{13,9},{6,2},{10,6},{14,10},{7,3},{... | collective-permute-start | bytes 92168 | tf_op jit(solution)/shard_map/ppermute | solution.py:25
  76.9 4.1 %collective-permute-start.9 = (f32[5,8,1,192]{3,1,2,0:T(8,128)S(1)}, f32[5,8,1,192]{3,1,2,0:T(8,128)S(1)}, u32[]{:S(2)}, u32[]{:S(2)}) collective-permute-start(f32[5,8,1,192]{3,1,2,0:T(8,128)S(1)} %get-tuple-element.12), channel_id=1, source_target_pairs={{0,4},{4,8},{8,12},{1,5},{5,9},{9,13},{2,6},{6,10},{10,14},{3,7},{... | collective-permute-start | bytes 92168 | tf_op jit(solution)/shard_map/ppermute | solution.py:24
  81.4 7.4 %collective-permute-start.11 = (f32[5,8,14,1]{3,1,2,0:T(8,128)S(1)}, f32[5,8,14,1]{3,1,2,0:T(8,128)S(1)}, u32[]{:S(2)}, u32[]{:S(2)}) collective-permute-start(f32[5,8,14,1]{3,1,2,0:T(8,128)S(1)} %get-tuple-element.17), channel_id=1, source_target_pairs={{0,1},{1,2},{2,3},{4,5},{5,6},{6,7},{8,9},{9,10},{10,11},{12,13},{... | collective-permute-start | bytes 6728 | tf_op jit(solution)/shard_map/ppermute | solution.py:24
  83.8 9.7 %collective-permute-start.10 = (f32[5,8,14,1]{3,1,2,0:T(8,128)S(1)}, f32[5,8,14,1]{3,1,2,0:T(8,128)S(1)}, u32[]{:S(2)}, u32[]{:S(2)}) collective-permute-start(f32[5,8,14,1]{3,1,2,0:T(8,128)S(1)} %get-tuple-element.16), channel_id=1, source_target_pairs={{1,0},{2,1},{3,2},{5,4},{6,5},{7,6},{9,8},{10,9},{11,10},{13,12},{... | collective-permute-start | bytes 6728 | tf_op jit(solution)/shard_map/ppermute | solution.py:25
  97.4 17.9 %copy-start.5 = (f32[64,128]{1,0:T(8,128)S(1)}, f32[64,128]{1,0:T(8,128)}, u32[]{:S(2)}) copy-start(f32[64,128]{1,0:T(8,128)} %get-tuple-element.27) | copy-start | bytes 98308
  97.4 17.9 %copy-start.6 = (f32[64,128]{1,0:T(8,128)S(1)}, f32[64,128]{1,0:T(8,128)}, u32[]{:S(2)}) copy-start(f32[64,128]{1,0:T(8,128)} %get-tuple-element.28) | copy-start | bytes 98308
  97.4 17.9 %copy-start.7 = (f32[64,128]{1,0:T(8,128)S(1)}, f32[64,128]{1,0:T(8,128)}, u32[]{:S(2)}) copy-start(f32[64,128]{1,0:T(8,128)} %get-tuple-element.30) | copy-start | bytes 98308
  97.4 17.9 %copy-start.8 = (f32[64,128]{1,0:T(8,128)S(1)}, f32[64,128]{1,0:T(8,128)}, u32[]{:S(2)}) copy-start(f32[64,128]{1,0:T(8,128)} %get-tuple-element.24) | copy-start | bytes 98308
  97.5 17.9 %copy-start.9 = (f32[64,128]{1,0:T(8,128)S(1)}, f32[64,128]{1,0:T(8,128)}, u32[]{:S(2)}) copy-start(f32[64,128]{1,0:T(8,128)} %get-tuple-element.25) | copy-start | bytes 98308
  97.5 17.9 %copy-start.10 = (f32[64,128]{1,0:T(8,128)S(1)}, f32[64,128]{1,0:T(8,128)}, u32[]{:S(2)}) copy-start(f32[64,128]{1,0:T(8,128)} %get-tuple-element.26) | copy-start | bytes 98308
where the time goes:
time: 144 us
  blocking collectives  53.4 us (37%)
  starting transfers between devices  30.3 us (21%)
  local copies, waits for them, and re-layouts  19.8 us (14%)
  matrix products  17.4 us (12%)
  waiting for transfers between devices  11.9 us (8%)
  other arithmetic  9.8 us (7%)
    psum x1, blocking collectives, on_device(): spectra = lax.psum(partial_sums, ('flow', 'col'))  25.7 us
    ppermute x6, starting transfers between devices, with_halo(): before = lax.ppermute(last, axis, up)  22.3 us
    all_gather x1, blocking collectives, on_device(): lax.all_gather(surface_samples, 'row', axis=2, tiled=True)  14.4 us
    all_gather x1, blocking collectives, on_device(): lax.all_gather(panel_points, 'row', axis=1, tiled=True)  13.2 us
    dot_general x12, matrix products, contract_small(): result = jnp.einsum('...p,qp->...q', blocked, matrix, precision=HIGH)  11.6 us
    ppermute x6, starting transfers between devices, with_halo(): after = lax.ppermute(first, axis, down)  7.92 us
    ppermute x6, waiting for transfers between devices, with_halo(): after = lax.ppermute(first, axis, down)  6.94 us
    mul x1, other arithmetic, on_device(): wide_back = jnp.kron(identity, eigen_bases[2])  4.95 us
  transfers between devices with their start and end apart: 12, of which 5 were waited for; matrix products, arithmetic and copies ran while one was open for 20% of the time, Pallas kernels for 0%

commit v1 on v0

--- a/solution.py
+++ b/solution.py
@@ -161,7 +161,7 @@
     source_re, source_im = transform(samples)
     own_obs = lax.dynamic_slice_in_dim(observers, lax.axis_index("row") * count, count, 1)
     partial_sums = far_terms(own_obs, points, source_re, source_im)
-    spectra = lax.psum(partial_sums, ("flow", "col"))
+    spectra = lax.psum(lax.psum(partial_sums, "col"), "flow")
     return (state, spectra)
 
 

time: 144 us -> 140 us (0.972)
  blocking collectives: 53.4 us -> 48.8 us
    psum x1 -> x2, blocking collectives: 25.7 us -> 21.1 us  [on_device(): spectra = lax.psum(lax.psum(partial_sums, 'col'), 'flow')]
where the time goes in v1:
time: 140 us; the launch traced here: 139 us
  blocking collectives  48.8 us (35%)
  starting transfers between devices  30.3 us (22%)
  local copies, waits for them, and re-layouts  19.8 us (14%)
  matrix products  17.4 us (12%)
  waiting for transfers between devices  11.8 us (8%)
  other arithmetic  9.8 us (7%)
    ppermute x6, starting transfers between devices, with_halo(): before = lax.ppermute(last, axis, up)  22.3 us
    psum x2, blocking collectives, on_device(): spectra = lax.psum(lax.psum(partial_sums, 'col'), 'flow')  21.1 us
    all_gather x1, blocking collectives, on_device(): lax.all_gather(surface_samples, 'row', axis=2, tiled=True)  14.5 us
    all_gather x1, blocking collectives, on_device(): lax.all_gather(panel_points, 'row', axis=1, tiled=True)  13.2 us
    dot_general x12, matrix products, contract_small(): result = jnp.einsum('...p,qp->...q', blocked, matrix, precision=HIGH)  11.6 us
    ppermute x6, starting transfers between devices, with_halo(): after = lax.ppermute(first, axis, down)  7.92 us
    ppermute x6, waiting for transfers between devices, with_halo(): after = lax.ppermute(first, axis, down)  6.94 us
    mul x1, other arithmetic, on_device(): wide_back = jnp.kron(identity, eigen_bases[2])  4.95 us
  transfers between devices with their start and end apart: 12, of which 5 were waited for; matrix products, arithmetic and copies ran while one was open for 20% of the time, Pallas kernels for 0%

profile of v1, /device:TPU:0, one launch (start us, length us, event | category | flops | bytes accessed | tf_op | source)
XLA Modules:
  0.0 139.2 jit_solution(3949858778457052444)
XLA Ops:
  0.6 0.9 fusion.168
  1.7 1.3 collective-permute-start
  3.0 4.8 %collective-permute-start.1 = (f32[5,1,12,192]{3,1,2,0:T(1,128)S(1)}, f32[5,1,12,192]{3,1,2,0:T(1,128)S(1)}, u32[]{:S(2)}, u32[]{:S(2)}) collective-permute-start(f32[5,1,12,192]{3,1,2,0:T(1,128)S(1)} %copy.139), channel_id=1, source_target_pairs={{0,16},{1,17},{2,18},{3,19},{4,20},{5,21},{6,22},{7,23},{8,24},{9,... | collective-permute-start | bytes 138248 | tf_op jit(solution)/shard_map/ppermute | solution.py:24
  7.9 1.3 copy.153
  9.2 0.7 slice_bitcast_fusion.12
  10.0 0.8 slice_bitcast_fusion.15
  10.8 0.9 fusion.131
  11.7 4.9 %broadcast_multiply_fusion = (f32[32,6,32,6]{3,2,1,0:T(8,128)}, f32[32,6,32,6]{3,2,1,0:T(8,128)}, f32[32,6,32,6]{3,2,1,0:T(8,128)}) fusion(f32[6,6]{1,0:T(8,128)S(1)} %get-tuple-element.42, f32[32,32]{1,0:T(8,128)S(1)} %fusion.118, f32[6,6]{1,0:T(8,128)S(1)} %copy.146, f32[6,6]{1,0:T(8,128)S(1)} %fusion.131), kind=kLoop, calls=%fused_computation | loop fusion | flops 110592 | bytes 446896 | tf_op jit(solution)/shard_map/jit(kron)/mul | solution.py:114
  16.6 3.9 %reshape.301 = f32[192,192,1,1]{1,0,2,3:T(8,128)S(1)} reshape(f32[32,6,32,6]{3,2,1,0:T(8,128)} %get-tuple-element.41) | data formatting | bytes 294912 | tf_op jit(solution)/shard_map/jit(kron)/mul | solution.py:112
  20.6 0.7 convolution_bitcast_fusion.6
  21.4 0.6 convolution_bitcast_fusion.7
  22.1 0.2 copy.134
  22.5 0.1 broadcast_in_dim.21
  22.9 13.2 %all-gather = f32[4,32,3]{1,2,0:T(4,128)S(1)} all-gather(f32[1,32,3]{1,2,0:T(4,128)S(1)} %bitcast.282), channel_id=1, replica_groups=mesh['flow'=2,'col'=4,'row'=4] {'row'}, dimensions={0}, use_global_device_ids=true | all-gather | bytes 1920 | tf_op jit(solution)/shard_map/all_gather | solution.py:158
  36.4 0.7 broadcast_multiply_fusion.3
  37.2 0.6 slice_bitcast_fusion.2
  37.8 0.7 add_add_fusion
  38.5 1.1 fusion.3
  39.7 1.3 collective-permute-start.2
  41.0 3.0 %collective-permute-start.3 = (f32[5,8,1,192]{3,1,2,0:T(8,128)S(1)}, f32[5,8,1,192]{3,1,2,0:T(8,128)S(1)}, u32[]{:S(2)}, u32[]{:S(2)}) collective-permute-start(f32[5,8,1,192]{3,1,2,0:T(8,128)S(1)} %get-tuple-element.14), channel_id=1, source_target_pairs={{0,4},{4,8},{8,12},{1,5},{5,9},{9,13},{2,6},{6,10},{10,14},{3,7},{... | collective-permute-start | bytes 92168 | tf_op jit(solution)/shard_map/ppermute | solution.py:24
  44.1 0.8 collective-permute-done.3
  44.9 0.2 pad_maximum_fusion
  45.2 4.2 %collective-permute-start.5 = (f32[5,8,14,1]{3,1,2,0:T(8,128)S(1)}, f32[5,8,14,1]{3,1,2,0:T(8,128)}, u32[]{:S(2)}, u32[]{:S(2)}) collective-permute-start(f32[5,8,14,1]{3,1,2,0:T(8,128)S(1)} %get-tuple-element.19), channel_id=1, source_target_pairs={{0,1},{1,2},{2,3},{4,5},{5,6},{6,7},{8,9},{9,10},{10,11},{12,13},{... | collective-permute-start | bytes 6728 | tf_op jit(solution)/shard_map/ppermute | solution.py:24
  49.5 1.5 %collective-permute-start.4 = (f32[5,8,14,1]{3,1,2,0:T(8,128)S(1)}, f32[5,8,14,1]{3,1,2,0:T(8,128)}, u32[]{:S(2)}, u32[]{:S(2)}) collective-permute-start(f32[5,8,14,1]{3,1,2,0:T(8,128)S(1)} %get-tuple-element.18), channel_id=1, source_target_pairs={{1,0},{2,1},{3,2},{5,4},{6,5},{7,6},{9,8},{10,9},{11,10},{13,12},{... | collective-permute-start | bytes 6728 | tf_op jit(solution)/shard_map/ppermute | solution.py:25
  50.9 3.9 %reshape.304 = f32[192,192,1,1]{1,0,2,3:T(8,128)S(1)} reshape(f32[32,6,32,6]{3,2,1,0:T(8,128)} %get-tuple-element.40) | data formatting | bytes 294912 | tf_op jit(solution)/shard_map/jit(kron)/mul | solution.py:113
  54.8 3.9 %reshape.307 = f32[192,192,1,1]{1,0,2,3:T(8,128)S(1)} reshape(f32[32,6,32,6]{3,2,1,0:T(8,128)} %get-tuple-element.39) | data formatting | bytes 294912 | tf_op jit(solution)/shard_map/jit(kron)/mul | solution.py:114
  58.8 2.2 %collective-permute-done.4 = f32[5,8,14,1]{3,1,2,0:T(8,128)} collective-permute-done((f32[5,8,14,1]{3,1,2,0:T(8,128)S(1)}, f32[5,8,14,1]{3,1,2,0:T(8,128)}, u32[]{:S(2)}, u32[]{:S(2)}) %collective-permute-start.4) | collective-permute-done | bytes 2272 | tf_op jit(solution)/shard_map/ppermute | solution.py:25
  61.0 2.7 %fusion.55 = f32[5,12,192,6]{2,3,1,0:T(8,128)S(1)} fusion(f32[5,6,12,192]{3,1,2,0:T(8,128)S(1)} %fusion.3, f32[5,8,14,1]{3,1,2,0:T(8,128)} %collective-permute-done.5, f32[5,8,1,192]{3,1,2,0:T(8,128)S(1)} %collective-permute-done.2, f32[5,8,1,192]{3,1,2,0:T(8,128)S(1)} %collective-permute-done.3, f32[5,1,12,192]{3,1,2,0:T(1,128)S(1)} %collective-permute-done, ...), kind=kOutput, calls=%fused_computation.96 | convolution fusion | flops 7119360 | bytes 1476992 | tf_op jit(solution)/shard_map/...p,qp->...q/dot_general | solution.py:35
  63.8 0.6 convolution_bitcast_fusion.5
  64.4 0.2 copy.145
  64.7 0.6 fusion.11
  65.3 0.8 fusion.90
  66.1 0.6 convolution_bitcast_fusion.4
  66.7 0.2 copy.150
  66.9 0.8 fusion.10
  67.9 1.3 collective-permute-start.6
  69.2 4.5 %collective-permute-start.7 = (f32[5,1,12,192]{3,1,2,0:T(1,128)S(1)}, f32[5,1,12,192]{3,1,2,0:T(1,128)S(1)}, u32[]{:S(2)}, u32[]{:S(2)}) collective-permute-start(f32[5,1,12,192]{3,1,2,0:T(1,128)S(1)} %get-tuple-element.20), channel_id=1, source_target_pairs={{0,16},{1,17},{2,18},{3,19},{4,20},{5,21},{6,22},{7,23},{8,24},{9,... | collective-permute-start | bytes 138248 | tf_op jit(solution)/shard_map/ppermute | solution.py:24
  73.7 0.6 fusion.114
  74.4 1.2 collective-permute-done.7
  75.6 1.3 collective-permute-start.8
  76.9 3.3 %collective-permute-start.9 = (f32[5,8,1,192]{3,1,2,0:T(8,128)S(1)}, f32[5,8,1,192]{3,1,2,0:T(8,128)S(1)}, u32[]{:S(2)}, u32[]{:S(2)}) collective-permute-start(f32[5,8,1,192]{3,1,2,0:T(8,128)S(1)} %get-tuple-element.12), channel_id=1, source_target_pairs={{0,4},{4,8},{8,12},{1,5},{5,9},{9,13},{2,6},{6,10},{10,14},{3,7},{... | collective-permute-start | bytes 92168 | tf_op jit(solution)/shard_map/ppermute | solution.py:24
  80.2 0.6 convolution_bitcast_fusion.2
  80.8 0.2 copy.155
  81.0 0.2 pad_maximum_fusion.1
  81.4 2.4 %collective-permute-start.11 = (f32[5,8,14,1]{3,1,2,0:T(8,128)S(1)}, f32[5,8,14,1]{3,1,2,0:T(8,128)S(1)}, u32[]{:S(2)}, u32[]{:S(2)}) collective-permute-start(f32[5,8,14,1]{3,1,2,0:T(8,128)S(1)} %get-tuple-element.17), channel_id=1, source_target_pairs={{0,1},{1,2},{2,3},{4,5},{5,6},{6,7},{8,9},{9,10},{10,11},{12,13},{... | collective-permute-start | bytes 6728 | tf_op jit(solution)/shard_map/ppermute | solution.py:24
  83.8 1.3 collective-permute-start.10
  85.1 0.8 fusion.7
  85.9 2.9 %collective-permute-done.11 = f32[5,8,14,1]{3,1,2,0:T(8,128)S(1)} collective-permute-done((f32[5,8,14,1]{3,1,2,0:T(8,128)S(1)}, f32[5,8,14,1]{3,1,2,0:T(8,128)S(1)}, u32[]{:S(2)}, u32[]{:S(2)}) %collective-permute-start.11) | collective-permute-done | bytes 2272 | tf_op jit(solution)/shard_map/ppermute | solution.py:24
  88.8 4.7 %collective-permute-done.10 = f32[5,8,14,1]{3,1,2,0:T(8,128)S(1)} collective-permute-done((f32[5,8,14,1]{3,1,2,0:T(8,128)S(1)}, f32[5,8,14,1]{3,1,2,0:T(8,128)S(1)}, u32[]{:S(2)}, u32[]{:S(2)}) %collective-permute-start.10) | collective-permute-done | bytes 2272 | tf_op jit(solution)/shard_map/ppermute | solution.py:25
  93.5 1.7 %fusion.28 = f32[5,12,192,6]{2,3,1,0:T(8,128)S(1)} fusion(f32[5,6,12,192]{3,1,2,0:T(8,128)S(1)} %fusion.7, f32[5,8,14,1]{3,1,2,0:T(8,128)S(1)} %collective-permute-done.11, f32[5,8,1,192]{3,1,2,0:T(8,128)S(1)} %collective-permute-done.8, f32[5,8,1,192]{3,1,2,0:T(8,128)S(1)} %collective-permute-done.9, f32[5,1,12,192]{3,1,2,0:T(1,128)S(1)} %collective-permute-done.6, ...), kind=kOutput, calls=%fused_computation.57 | convolution fusion | flops 7119360 | bytes 2045952 | tf_op jit(solution)/shard_map/...p,qp->...q/dot_general | solution.py:35
  95.2 0.6 convolution_bitcast_fusion.1
  95.8 0.2 copy.162
  96.0 0.6 fusion.9
  96.6 0.8 fusion.84
  97.5 0.6 convolution_bitcast_fusion
  98.1 0.2 copy.166
  98.3 0.7 fusion.8
  99.0 0.9 copy.174
  100.1 14.5 %all_gather.7 = f32[4,16,128]{1,0,2:T(4,128)S(1)} all-gather(f32[4,16,32]{1,0,2:T(4,128)S(1)} %pad_maximum_fusion.62), channel_id=1, replica_groups=mesh['flow'=2,'col'=4,'row'=4] {'row'}, dimensions={2}, use_global_device_ids=true | all-gather | bytes 40960 | tf_op jit(solution)/shard_map/all_gather | solution.py:159
  114.7 0.3 convolution_bitcast_fusion.9
  115.0 0.3 fusion.12
  115.3 2.7 %fusion.17 = (f32[16,64]{1,0:T(8,128)S(1)}, f32[16,64]{1,0:T(8,128)S(1)}) fusion(f32[16,128]{1,0:T(8,128)S(1)} %get-tuple-element.36, f32[64,128]{1,0:T(8,128)S(1)} %copy-done.6, f32[64,128]{1,0:T(8,128)S(1)} %copy-done.7, f32[16,128]{1,0:T(8,128)S(1)} %get-tuple-element.37, f32[16,128]{1,0:T(8,128)S(1)} %get-tuple-element.38, ...), kind=kLoop, calls=%fused_computation.41 | loop fusion | flops 3799040 | bytes 303232 | tf_op jit(solution)/shard_map/reduce_sum | solution.py:76
  118.1 11.5 %psum.14 = f32[2,16,64]{2,1,0:T(8,128)S(1)} all-reduce(f32[2,16,64]{2,1,0:T(8,128)S(1)} %pad_maximum_fusion.69), channel_id=1, replica_groups=mesh['flow'=2,'col'=4,'row'=4] {'col'}, use_global_device_ids=true, to_apply=%region_3.4 | all-reduce | flops 2048 | bytes 16384 | tf_op jit(solution)/shard_map/psum | solution.py:164
  129.6 9.6 %psum.15 = f32[2,16,64]{2,1,0:T(8,128)} all-reduce(f32[2,16,64]{2,1,0:T(8,128)S(1)} %psum.14), channel_id=1, replica_groups=mesh['flow'=2,'col'=4,'row'=4] {'flow'}, use_global_device_ids=true, to_apply=%region_4.5 | all-reduce | flops 2048 | bytes 16384 | tf_op jit(solution)/shard_map/psum | solution.py:164
  (71 shorter events, 2.1 us)
Async XLA Ops:
  0.6 35.6 %copy-start = (f32[3,256]{1,0:T(4,128)S(1)}, f32[3,256]{1,0:T(4,128)}, u32[]{:S(2)}) copy-start(f32[3,256]{1,0:T(4,128)} %param.13) | copy-start | bytes 9220
  1.7 38.0 %collective-permute-start = (f32[5,1,12,192]{3,1,2,0:T(1,128)S(1)}, f32[5,1,12,192]{3,1,2,0:T(1,128)S(1)}, u32[]{:S(2)}, u32[]{:S(2)}) collective-permute-start(f32[5,1,12,192]{3,1,2,0:T(1,128)S(1)} %copy.137), channel_id=1, source_target_pairs={{16,0},{17,1},{18,2},{19,3},{20,4},{21,5},{22,6},{23,7},{24,8},{25... | collective-permute-start | bytes 138248 | tf_op jit(solution)/shard_map/ppermute | solution.py:25
  3.0 36.6 %collective-permute-start.1 = (f32[5,1,12,192]{3,1,2,0:T(1,128)S(1)}, f32[5,1,12,192]{3,1,2,0:T(1,128)S(1)}, u32[]{:S(2)}, u32[]{:S(2)}) collective-permute-start(f32[5,1,12,192]{3,1,2,0:T(1,128)S(1)} %copy.139), channel_id=1, source_target_pairs={{0,16},{1,17},{2,18},{3,19},{4,20},{5,21},{6,22},{7,23},{8,24},{9,... | collective-permute-start | bytes 138248 | tf_op jit(solution)/shard_map/ppermute | solution.py:24
  16.6 4.0 %copy-start.1 = (f32[5,6,12,192]{3,2,1,0:T(8,128)S(1)}, f32[5,6,12,192]{3,2,1,0:T(8,128)}, u32[]{:S(2)}) copy-start(f32[5,6,12,192]{3,2,1,0:T(8,128)} %param.9) | copy-start | bytes 829444
  16.6 4.7 %copy-start.3 = (f32[3,6,6]{2,1,0:T(8,128)S(1)}, f32[3,6,6]{2,1,0:T(8,128)}, u32[]{:S(2)}) copy-start(f32[3,6,6]{2,1,0:T(8,128)} %param.11) | copy-start | bytes 1300
  16.6 5.8 %copy-start.13 = (f32[1,2,32]{2,1,0:T(2,128)S(1)}, f32[1,2,32]{2,1,0:T(2,128)}, u32[]{:S(2)}) copy-start(f32[1,2,32]{2,1,0:T(2,128)} %param.10) | copy-start | bytes 772
  16.6 6.3 %copy-start.12 = (f32[3,32]{1,0:T(4,128)S(1)}, f32[3,32]{1,0:T(4,128)}, u32[]{:S(2)}) copy-start(f32[3,32]{1,0:T(4,128)} %param.14) | copy-start | bytes 1156
  16.6 21.9 %copy-start.2 = (f32[5,6,12,192]{3,2,1,0:T(8,128)S(1)}, f32[5,6,12,192]{3,2,1,0:T(8,128)}, u32[]{:S(2)}) copy-start(f32[5,6,12,192]{3,2,1,0:T(8,128)} %param.8) | copy-start | bytes 829444
  39.7 4.4 %collective-permute-start.2 = (f32[5,8,1,192]{3,1,2,0:T(8,128)S(1)}, f32[5,8,1,192]{3,1,2,0:T(8,128)S(1)}, u32[]{:S(2)}, u32[]{:S(2)}) collective-permute-start(f32[5,8,1,192]{3,1,2,0:T(8,128)S(1)} %get-tuple-element.15), channel_id=1, source_target_pairs={{4,0},{8,4},{12,8},{5,1},{9,5},{13,9},{6,2},{10,6},{14,10},{7,3},{... | collective-permute-start | bytes 92168 | tf_op jit(solution)/shard_map/ppermute | solution.py:25
  41.0 3.9 %collective-permute-start.3 = (f32[5,8,1,192]{3,1,2,0:T(8,128)S(1)}, f32[5,8,1,192]{3,1,2,0:T(8,128)S(1)}, u32[]{:S(2)}, u32[]{:S(2)}) collective-permute-start(f32[5,8,1,192]{3,1,2,0:T(8,128)S(1)} %get-tuple-element.14), channel_id=1, source_target_pairs={{0,4},{4,8},{8,12},{1,5},{5,9},{9,13},{2,6},{6,10},{10,14},{3,7},{... | collective-permute-start | bytes 92168 | tf_op jit(solution)/shard_map/ppermute | solution.py:24
  45.2 13.5 %collective-permute-start.5 = (f32[5,8,14,1]{3,1,2,0:T(8,128)S(1)}, f32[5,8,14,1]{3,1,2,0:T(8,128)}, u32[]{:S(2)}, u32[]{:S(2)}) collective-permute-start(f32[5,8,14,1]{3,1,2,0:T(8,128)S(1)} %get-tuple-element.19), channel_id=1, source_target_pairs={{0,1},{1,2},{2,3},{4,5},{5,6},{6,7},{8,9},{9,10},{10,11},{12,13},{... | collective-permute-start | bytes 6728 | tf_op jit(solution)/shard_map/ppermute | solution.py:24
  49.5 11.6 %collective-permute-start.4 = (f32[5,8,14,1]{3,1,2,0:T(8,128)S(1)}, f32[5,8,14,1]{3,1,2,0:T(8,128)}, u32[]{:S(2)}, u32[]{:S(2)}) collective-permute-start(f32[5,8,14,1]{3,1,2,0:T(8,128)S(1)} %get-tuple-element.18), channel_id=1, source_target_pairs={{1,0},{2,1},{3,2},{5,4},{6,5},{7,6},{9,8},{10,9},{11,10},{13,12},{... | collective-permute-start | bytes 6728 | tf_op jit(solution)/shard_map/ppermute | solution.py:25
  50.9 7.7 %copy-start.11 = (f32[4,15,32]{2,0,1:T(4,128)S(1)}, f32[4,15,32]{2,0,1:T(4,128)}, u32[]{:S(2)}) copy-start(f32[4,15,32]{2,0,1:T(4,128)} %param.15) | copy-start | bytes 23044
  61.0 3.6 %copy-start.4 = (f32[6,12,192]{2,1,0:T(8,128)S(1)}, f32[6,12,192]{2,1,0:T(8,128)}, u32[]{:S(2)}) copy-start(f32[6,12,192]{2,1,0:T(8,128)} %add_add_fusion) | copy-start | bytes 165892
  67.9 6.5 %collective-permute-start.6 = (f32[5,1,12,192]{3,1,2,0:T(1,128)S(1)}, f32[5,1,12,192]{3,1,2,0:T(1,128)S(1)}, u32[]{:S(2)}, u32[]{:S(2)}) collective-permute-start(f32[5,1,12,192]{3,1,2,0:T(1,128)S(1)} %get-tuple-element.21), channel_id=1, source_target_pairs={{16,0},{17,1},{18,2},{19,3},{20,4},{21,5},{22,6},{23,7},{24,8},{25... | collective-permute-start | bytes 138248 | tf_op jit(solution)/shard_map/ppermute | solution.py:25
  69.2 6.4 %collective-permute-start.7 = (f32[5,1,12,192]{3,1,2,0:T(1,128)S(1)}, f32[5,1,12,192]{3,1,2,0:T(1,128)S(1)}, u32[]{:S(2)}, u32[]{:S(2)}) collective-permute-start(f32[5,1,12,192]{3,1,2,0:T(1,128)S(1)} %get-tuple-element.20), channel_id=1, source_target_pairs={{0,16},{1,17},{2,18},{3,19},{4,20},{5,21},{6,22},{7,23},{8,24},{9,... | collective-permute-start | bytes 138248 | tf_op jit(solution)/shard_map/ppermute | solution.py:24
  75.6 5.4 %collective-permute-start.8 = (f32[5,8,1,192]{3,1,2,0:T(8,128)S(1)}, f32[5,8,1,192]{3,1,2,0:T(8,128)S(1)}, u32[]{:S(2)}, u32[]{:S(2)}) collective-permute-start(f32[5,8,1,192]{3,1,2,0:T(8,128)S(1)} %get-tuple-element.13), channel_id=1, source_target_pairs={{4,0},{8,4},{12,8},{5,1},{9,5},{13,9},{6,2},{10,6},{14,10},{7,3},{... | collective-permute-start | bytes 92168 | tf_op jit(solution)/shard_map/ppermute | solution.py:25
  76.9 4.1 %collective-permute-start.9 = (f32[5,8,1,192]{3,1,2,0:T(8,128)S(1)}, f32[5,8,1,192]{3,1,2,0:T(8,128)S(1)}, u32[]{:S(2)}, u32[]{:S(2)}) collective-permute-start(f32[5,8,1,192]{3,1,2,0:T(8,128)S(1)} %get-tuple-element.12), channel_id=1, source_target_pairs={{0,4},{4,8},{8,12},{1,5},{5,9},{9,13},{2,6},{6,10},{10,14},{3,7},{... | collective-permute-start | bytes 92168 | tf_op jit(solution)/shard_map/ppermute | solution.py:24
  81.4 7.4 %collective-permute-start.11 = (f32[5,8,14,1]{3,1,2,0:T(8,128)S(1)}, f32[5,8,14,1]{3,1,2,0:T(8,128)S(1)}, u32[]{:S(2)}, u32[]{:S(2)}) collective-permute-start(f32[5,8,14,1]{3,1,2,0:T(8,128)S(1)} %get-tuple-element.17), channel_id=1, source_target_pairs={{0,1},{1,2},{2,3},{4,5},{5,6},{6,7},{8,9},{9,10},{10,11},{12,13},{... | collective-permute-start | bytes 6728 | tf_op jit(solution)/shard_map/ppermute | solution.py:24
  83.8 9.7 %collective-permute-start.10 = (f32[5,8,14,1]{3,1,2,0:T(8,128)S(1)}, f32[5,8,14,1]{3,1,2,0:T(8,128)S(1)}, u32[]{:S(2)}, u32[]{:S(2)}) collective-permute-start(f32[5,8,14,1]{3,1,2,0:T(8,128)S(1)} %get-tuple-element.16), channel_id=1, source_target_pairs={{1,0},{2,1},{3,2},{5,4},{6,5},{7,6},{9,8},{10,9},{11,10},{13,12},{... | collective-permute-start | bytes 6728 | tf_op jit(solution)/shard_map/ppermute | solution.py:25
  97.4 17.9 %copy-start.5 = (f32[64,128]{1,0:T(8,128)S(1)}, f32[64,128]{1,0:T(8,128)}, u32[]{:S(2)}) copy-start(f32[64,128]{1,0:T(8,128)} %get-tuple-element.27) | copy-start | bytes 98308
  97.4 17.9 %copy-start.6 = (f32[64,128]{1,0:T(8,128)S(1)}, f32[64,128]{1,0:T(8,128)}, u32[]{:S(2)}) copy-start(f32[64,128]{1,0:T(8,128)} %get-tuple-element.28) | copy-start | bytes 98308
  97.4 17.9 %copy-start.7 = (f32[64,128]{1,0:T(8,128)S(1)}, f32[64,128]{1,0:T(8,128)}, u32[]{:S(2)}) copy-start(f32[64,128]{1,0:T(8,128)} %get-tuple-element.30) | copy-start | bytes 98308
  97.4 17.9 %copy-start.8 = (f32[64,128]{1,0:T(8,128)S(1)}, f32[64,128]{1,0:T(8,128)}, u32[]{:S(2)}) copy-start(f32[64,128]{1,0:T(8,128)} %get-tuple-element.24) | copy-start | bytes 98308
  97.4 17.9 %copy-start.9 = (f32[64,128]{1,0:T(8,128)S(1)}, f32[64,128]{1,0:T(8,128)}, u32[]{:S(2)}) copy-start(f32[64,128]{1,0:T(8,128)} %get-tuple-element.25) | copy-start | bytes 98308
  97.4 17.9 %copy-start.10 = (f32[64,128]{1,0:T(8,128)S(1)}, f32[64,128]{1,0:T(8,128)}, u32[]{:S(2)}) copy-start(f32[64,128]{1,0:T(8,128)} %get-tuple-element.26) | copy-start | bytes 98308
